TPU v7x, 32 devices: a whole 2x2x4 slice. The times are simulated.
32 devices in a mesh: row: 8 (over y, x, core), col: 4 (over z).
Axes of the slice: x: 2, y: 2, z: 4, core: 2. Of those that a mesh axis runs over, the one named last changes fastest.
Arguments:
- head_points: float32 [8, 2, 1024], P(None, None, 'row'), may hold values from 0 to 1
- tail_points: float32 [8, 8192], P(None, 'row'), may hold values from 0 to 1
- eval_points: float32 [8, 4096], P(None, 'col'), may hold values from 0 to 1
- length_scales: float32 [8], replicated, may hold values from 0.5 to 2
- head_factor: float32 [2, 1024, 2, 1024], P(None, 'row', None, 'col'), as said below
- tail_factor: float32 [8192, 2, 1024], P('row', None, 'col'), may hold values from -0.125 to 0.125
Outputs:
- head_solved: float32 [2, 1024, 4096], P(None, 'row', 'col')
- tail_rhs: float32 [8192, 4096], P('row', 'col')
Inputs may be any that keep to these rules, and one draw needn't show every extreme that they name: head_factor[p, :, q, :] is zero for q > p; the blocks with p = q are lower triangular with a diagonal between 1 and 2.
All inputs are finite; a program needn't handle non-finite values.
Results may differ from a plain program's by a relative error of at most 0.00011.
Values sent between devices are 32-bit elements; how exact they have to be, the bound alone decides.
A program may use at most 192 MiB of HBM per device.

v0:
```python
import jax
import jax.numpy as jnp
from jax import lax
from jax.sharding import PartitionSpec as P


def kernel_block(row_points, col_points, length_scales):
    total = jnp.zeros((row_points.shape[1], col_points.shape[1]), jnp.float32)
    for dimension in range(row_points.shape[0]):
        spread = (row_points[dimension][:, None] - col_points[dimension][None, :]) / length_scales[
            dimension
        ]
        total = total + spread * spread
    scaled = jnp.sqrt(5.0 * total)
    return (1.0 + scaled + scaled * scaled / 3.0) * jnp.exp(-scaled)


def whole_triangle(block):
    band = lax.all_gather(block, "col", axis=1, tiled=True)
    return lax.all_gather(band, "row", axis=0, tiled=True)


def solve_panel(block, right_side):
    triangle = whole_triangle(block)
    spread = lax.all_to_all(right_side, "row", split_axis=1, concat_axis=0, tiled=True)
    partial_value = jax.scipy.linalg.solve_triangular(triangle, spread, lower=True)
    return lax.all_gather(partial_value, "row", axis=1, tiled=True)


def apply_panel(rows_factor, solved):
    return jnp.dot(
        lax.all_gather(rows_factor, "col", axis=1, tiled=True),
        solved,
        precision=lax.Precision.HIGHEST,
        preferred_element_type=jnp.float32,
    )


def per_device(head_points, tail_points, eval_points, length_scales, head_factor, tail_factor):
    panel_rows = head_factor.shape[1]
    row_index = lax.axis_index("row")
    second = kernel_block(head_points[:, 1, :], eval_points, length_scales)
    tail = kernel_block(tail_points, eval_points, length_scales)
    first = kernel_block(head_points[:, 0, :], eval_points, length_scales)
    solved_one = solve_panel(head_factor[0, :, 0, :], first)
    update_rows = jnp.concatenate([head_factor[1, :, 0, :], tail_factor[:, 0, :]], 0)
    change = apply_panel(update_rows, solved_one)
    second_rhs = second - change[:panel_rows]
    tail = tail - change[panel_rows:]
    solved_two = solve_panel(head_factor[1, :, 1, :], second_rhs)
    tail = tail - apply_panel(tail_factor[:, 1, :], solved_two)
    local_one = lax.dynamic_slice_in_dim(solved_one, row_index * panel_rows, panel_rows, 0)
    local_two = lax.dynamic_slice_in_dim(solved_two, row_index * panel_rows, panel_rows, 0)
    return (jnp.stack([local_one, local_two]), tail)


def solution(mesh):
    placed = (
        P(None, None, "row"),
        P(None, "row"),
        P(None, "col"),
        P(),
        P(None, "row", None, "col"),
        P("row", None, "col"),
    )
    return jax.shard_map(
        per_device,
        mesh=mesh,
        in_specs=placed,
        out_specs=(P(None, "row", "col"), P("row", "col")),
        check_vma=False,
    )
```

profile of v0, /device:TPU:0, one launch (start us, length us, event | category | flops | bytes accessed | tf_op | source)
XLA Modules:
  0.0 490.4 jit_solution(16541988839072723393)
XLA Ops:
  8.8 18.0 %all-gather = f32[1,128,1,1024]{3,1,2,0:T(8,128)} all-gather(f32[1,128,1,256]{3,1,2,0:T(8,128)S(1)} %copy.19), channel_id=2, replica_groups=mesh['row'=8,'col'=4] {'col'}, dimensions={3}, use_global_device_ids=true | all-gather | bytes 655360 | tf_op jit(solution)/shard_map/all_gather | solution.py:19
  26.9 17.2 %all-gather.2 = f32[1,128,1,1024]{3,1,2,0:T(8,128)} all-gather(f32[1,128,1,256]{3,1,2,0:T(8,128)S(1)} %copy.20), channel_id=4, replica_groups=mesh['row'=8,'col'=4] {'col'}, dimensions={3}, use_global_device_ids=true | all-gather | bytes 655360 | tf_op jit(solution)/shard_map/all_gather | solution.py:19
  47.8 6.8 %exponential_multiply_fusion = f32[128,8,128]{2,0,1:T(8,128)} fusion(f32[]{:T(128)} %bitcast.25, f32[8,128]{1,0:T(8,128)S(1)} %bitcast.250, f32[128]{0:T(128)S(1)} %get-tuple-element.120, f32[]{:T(128)} %bitcast.22, f32[8,128]{1,0:T(8,128)S(1)} %bitcast.253, f32[128]{0:T(128)S(1)} %get-tuple-element.121, f32[]{:T(128)} %bitcast.19, ...), kind=kLoop, calls=%fused_computation.33 | loop fusion | flops 4980736 | bytes 561184 | tf_op jit(solution)/shard_map/mul | solution.py:15
  54.6 3.7 all-to-all-start
  58.4 11.2 %all-gather.18.cloned.1.call-done = f32[1,1024,1,1024]{3,1,2,0:T(8,128)} async-done(((f32[1,128,1,1024]{3,1,2,0:T(8,128)}), f32[1,1024,1,1024]{3,1,2,0:T(8,128)}) %all-gather.18.cloned.1.call-update) | async-done | bytes 4194320 | tf_op jit(solution)/shard_map/all_gather | solution.py:20
  69.6 4.8 bitcast_select_fusion.1
  74.4 23.9 %while.4 = (s32[]{:T(128)}, f32[1024,1024]{1,0:T(8,128)}, s32[8,2]{0,1:T(2,128)S(1)}, f32[8,128,128]{2,1,0:T(8,128)S(1)}, s32[]{:T(128)}) while((s32[]{:T(128)}, f32[1024,1024]{1,0:T(8,128)}, s32[8,2]{0,1:T(2,128)S(1)}, f32[8,128,128]{2,1,0:T(8,128)S(1)}, s32[]{:T(128)}) %tuple.124), condition=%wide.while_cond, body=%wide.while_body.sunk | while | flops 2 | bytes 131189 | solution.py:26
  75.0 2.3 bitcast_dynamic-update-slice_fusion.4
  78.0 2.3 bitcast_dynamic-update-slice_fusion.4
  87.0 2.3 bitcast_dynamic-update-slice_fusion.4
  90.0 2.3 bitcast_dynamic-update-slice_fusion.4
  93.0 2.4 bitcast_dynamic-update-slice_fusion.4
  98.2 78.6 %custom-call.4 = f32[8,128,128]{1,2,0:T(8,128)S(1)} custom-call(f32[8,128,128]{2,1,0:T(8,128)S(1)} %get-tuple-element.17), custom_call_target="InvertDiagBlocksLowerTriangular" | custom-call | tf_op jit(solution)/shard_map/jit(_solve_triangular)/triangular_solve | solution.py:26
  190.8 4.8 bitcast_select_fusion
  195.6 5.6 %all-gather.14.cloned.1.call-done = f32[1152,1024]{1,0:T(8,128)} async-done(((f32[1152,256]{1,0:T(8,128)}), f32[1152,1024]{1,0:T(8,128)}) %all-gather.14.cloned.1.call-update) | async-done | bytes 4718608 | tf_op jit(solution)/shard_map/all_gather | solution.py:32
  201.2 37.6 %all-gather.12.cloned.1.call-done = f32[1024,1024]{1,0:T(8,128)} async-done(((f32[1024,128]{1,0:T(8,128)}), f32[1024,1024]{1,0:T(8,128)}) %all-gather.12.cloned.1.call-update) | async-done | bytes 4194320 | tf_op jit(solution)/shard_map/all_gather | solution.py:27
  238.8 21.3 %fusion.78 = f32[1152,1024]{0,1:T(8,128)S(1)} fusion(f32[1152,1024]{1,0:T(8,128)} %all-gather.14.cloned.1.call-done, f32[1024,1024]{1,0:T(8,128)} %all-gather.12.cloned.1.call-done), kind=kOutput, calls=%fused_computation.191 | convolution fusion | flops 14495514624 | bytes 13631488 | tf_op jit(solution)/shard_map/dot_general | solution.py:31
  262.3 6.4 %slice_subtract_fusion.1 = f32[128,1024]{0,1:T(8,128)S(1)} fusion(f32[1152,1024]{0,1:T(8,128)S(1)} %fusion.78, f32[]{:T(128)} %bitcast.25, f32[1024]{0:T(1024)S(1)} %bitcast.251, f32[128]{0:T(128)S(1)} %get-tuple-element.128, f32[]{:T(128)} %bitcast.22, f32[1024]{0:T(1024)S(1)} %bitcast.254, f32[128]{0:T(128)S(1)} %get-tuple-element.129, f32[]{:T(128)} %bitcast.19, ...), kind=kLoop, calls=%fused_computation.30 | loop fusion | flops 5111808 | bytes 1085472 | tf_op jit(solution)/shard_map/sub | solution.py:48
  269.7 3.5 all-to-all-start.1
  273.3 23.1 %while.5 = (s32[]{:T(128)}, f32[1024,1024]{1,0:T(8,128)}, s32[8,2]{0,1:T(2,128)S(1)}, f32[8,128,128]{2,1,0:T(8,128)S(1)}, s32[]{:T(128)}) while((s32[]{:T(128)}, f32[1024,1024]{1,0:T(8,128)}, s32[8,2]{0,1:T(2,128)S(1)}, f32[8,128,128]{2,1,0:T(8,128)S(1)}, s32[]{:T(128)}) %tuple.142), condition=%wide.while_cond.clone, body=%wide.while_body.clone.sunk | while | flops 2 | bytes 131189 | solution.py:26
  296.4 78.6 %custom-call.5 = f32[8,128,128]{1,2,0:T(8,128)S(1)} custom-call(f32[8,128,128]{2,1,0:T(8,128)S(1)} %get-tuple-element.18), custom_call_target="InvertDiagBlocksLowerTriangular" | custom-call | tf_op jit(solution)/shard_map/jit(_solve_triangular)/triangular_solve | solution.py:26
  388.7 37.7 %all-gather.16.cloned.1.call-done = f32[1024,1024]{1,0:T(8,128)} async-done(((f32[1024,128]{1,0:T(8,128)}), f32[1024,1024]{1,0:T(8,128)}) %all-gather.16.cloned.1.call-update) | async-done | bytes 4194320 | tf_op jit(solution)/shard_map/all_gather | solution.py:27
  426.5 49.4 %fusion = f32[1024,1024]{0,1:T(8,128)} fusion(f32[1152,1024]{0,1:T(8,128)} %copy-done.3, f32[]{:T(128)} %bitcast.25, f32[1024]{0:T(1024)S(1)} %bitcast.252, f32[1024]{0:T(1024)S(1)} %bitcast.262, f32[]{:T(128)} %bitcast.22, f32[1024]{0:T(1024)S(1)} %bitcast.255, f32[1024]{0:T(1024)S(1)} %bitcast.263, f32[]{:T(128)} %bitcast.19, f32[1024]{0:T(1024)S(1)} %bitcast.237, ...), kind=kOutput, calls=%fused_computation.5 | convolution fusion | flops 12926844928 | bytes 16842784 | tf_op jit(solution)/shard_map/dot_general | solution.py:31
  475.9 5.3 %copy.18 = f32[1024,1024]{1,0:T(8,128)} copy(f32[1024,1024]{0,1:T(8,128)} %fusion) | data formatting | bytes 8388608
  (125 shorter events, 73.2 us)
Async XLA Ops:
  7.2 37.1 %copy-start = (f32[1024,2,256]{2,1,0:T(2,128)S(1)}, f32[1024,2,256]{2,1,0:T(2,128)}, u32[]{:S(2)}) copy-start(f32[1024,2,256]{2,1,0:T(2,128)} %param.13) | copy-start | bytes 6291460
  7.2 62.4 %all-gather.18.cloned.1.call-start = ((), (), s32[]{:S(2)}) async-start(), calls=%async_computation.5 | async-start | bytes 4718592 | tf_op jit(solution)/shard_map/all_gather | solution.py:20
  26.8 163.9 %all-gather.20.cloned.1.call-start = ((), (), s32[]{:S(2)}) async-start(), calls=%async_computation.6 | async-start | bytes 4718592 | tf_op jit(solution)/shard_map/all_gather | solution.py:20
  44.1 2.9 copy-start.6
  44.2 3.6 copy-start.4
  44.2 3.6 copy-start.7
  44.2 157.0 %all-gather.14.cloned.1.call-start = ((), (), s32[]{:S(2)}) async-start(), calls=%async_computation.3 | async-start | bytes 5898240 | tf_op jit(solution)/shard_map/all_gather | solution.py:32
  54.6 122.2 %all-to-all-start = ((f32[128,8,128]{2,0,1:T(8,128)}), f32[128,8,128]{2,0,1:T(8,128)S(1)}, u32[]{:S(2)}, u32[]{:S(2)}) async-start(f32[128,8,128]{2,0,1:T(8,128)} %exponential_multiply_fusion), calls=%async_computation | async-start | bytes 1048576 | tf_op jit(solution)/shard_map/all_to_all | solution.py:25
  58.3 180.5 %all-gather.12.cloned.1.call-start = ((), (), s32[]{:S(2)}) async-start(), calls=%async_computation.2 | async-start | bytes 4718592 | tf_op jit(solution)/shard_map/all_gather | solution.py:27
  188.6 0.8 copy-start.1
  189.4 199.3 %all-gather.22.cloned.1.call-start = ((), (), s32[]{:S(2)}) async-start(), calls=%async_computation.7 | async-start | bytes 5242880 | tf_op jit(solution)/shard_map/all_gather | solution.py:32
  260.1 2.2 copy-start.3
  269.7 105.3 %all-to-all-start.1 = ((f32[128,8,128]{2,0,1:T(8,128)}), f32[128,8,128]{2,0,1:T(8,128)S(1)}, u32[]{:S(2)}, u32[]{:S(2)}) async-start(f32[128,8,128]{2,0,1:T(8,128)} %copy.16), calls=%async_computation.1 | async-start | bytes 1048576 | tf_op jit(solution)/shard_map/all_to_all | solution.py:25
  273.2 153.3 %all-gather.16.cloned.1.call-start = ((), (), s32[]{:S(2)}) async-start(), calls=%async_computation.4 | async-start | bytes 4718592 | tf_op jit(solution)/shard_map/all_gather | solution.py:27
  296.4 91.2 %copy-start.5 = (f32[8,1024]{1,0:T(8,128)S(1)}, f32[8,1024]{1,0:T(8,128)}, u32[]{:S(2)}) copy-start(f32[8,1024]{1,0:T(8,128)} %param.9) | copy-start | bytes 98308
  386.8 0.8 copy-start.2
Sparse Core Ops, SparseCore 0:
  27.0 42.5 all-gather.17
  71.4 38.5 all-gather.19
  111.6 89.5 all-gather.13
  202.9 35.8 all-gather.11
  240.8 80.7 all-gather.21
  387.7 38.7 all-gather.15
where the time goes:
time: 495 us; the launch traced here: 490 us
  other arithmetic  182 us (37%)
  matrix products  93.9 us (19%)
  waiting for transfers between devices  92.3 us (19%)
  local copies, waits for them, and re-layouts  64.1 us (13%)
  blocking collectives  35.2 us (7%)
  between operations  14.8 us (3%)
  starting transfers between devices  7.71 us (2%)
    another operation x5, other arithmetic, solve_panel(): jax.scipy.linalg.solve_triangular(triangle, spread, lower=True)  167 us
    all_gather x2, waiting for transfers between devices, solve_panel(): return lax.all_gather(partial_value, 'row', axis=1, tiled=True)  75.4 us
    dot_general x2, matrix products, apply_panel(): jnp.dot(lax.all_gather(rows_factor, 'col', axis=1, tiled=True), solved, p...  70.7 us
    another operation x51, local copies, waits for them, and re-layouts, solve_panel(): jax.scipy.linalg.solve_triangular(triangle, spread, lower=True)  46.7 us
    all_gather x2, blocking collectives, whole_triangle(): band = lax.all_gather(block, 'col', axis=1, tiled=True)  35.2 us
    another operation x30, matrix products, solve_panel(): jax.scipy.linalg.solve_triangular(triangle, spread, lower=True)  23.3 us
    all_gather x2, waiting for transfers between devices, whole_triangle(): return lax.all_gather(band, 'row', axis=0, tiled=True)  11.2 us
    unnamed x22, local copies, waits for them, and re-layouts  10.2 us
  transfers between devices with their start and end apart: 8, of which 4 were waited for; matrix products, arithmetic and copies ran while one was open for 57% of the time, Pallas kernels for 0%

commit v1 on v0

--- a/solution.py
+++ b/solution.py
@@ -1,7 +1,323 @@
+import functools
+
 import jax
 import jax.numpy as jnp
 from jax import lax
+from jax.experimental import pallas as pl
+from jax.experimental.pallas import tpu as pltpu
 from jax.sharding import PartitionSpec as P
+
+MESH = pl.DeviceIdType.MESH
+HIGHEST = lax.Precision.HIGHEST
+NB = 128
+
+
+def dot(a, b):
+    return jnp.dot(a, b, precision=HIGHEST, preferred_element_type=jnp.float32)
+
+
+def matern(rows, columns):
+    total = jnp.zeros((rows.shape[0], columns.shape[1]), jnp.float32)
+    for d in range(columns.shape[0]):
+        spread = rows[:, d : d + 1] - columns[d : d + 1, :]
+        total = total + spread * spread
+    s = jnp.sqrt(5.0 * total)
+    return (1.0 + s + s * s * (1.0 / 3.0)) * jnp.exp(-s)
+
+
+def inverse(block):
+    n = block.shape[0]
+    i = lax.broadcasted_iota(jnp.int32, (n, n), 0)
+    j = lax.broadcasted_iota(jnp.int32, (n, n), 1)
+    eye = i == j
+    diagonal = jnp.sum(jnp.where(eye, block, 0.0), axis=1, keepdims=True)
+    result = jnp.where(eye, 1.0 / diagonal, 0.0)
+    size = 1
+    while size < n:
+        pair = (i // (2 * size) == j // (2 * size)) & ((i // size) % 2 == 1) & ((j // size) % 2 == 0)
+        below = jnp.where(pair, block, 0.0)
+        result = result - dot(result, dot(below, result))
+        size *= 2
+    return result
+
+
+def kernel(
+    cols, hp_ref, tp_ref, ev_ref, lh_ref, f_ref, head_out, tail_out,
+    hp, l0, l1, x0, x1, rhs, fall, xhi, xlo, own_sem, ex_send, ex_recv, z_send, z_recv,
+):
+    r = lax.axis_index("row")
+    c = lax.axis_index("col")
+    sib = r + 1 - 2 * (r % 2)
+    across = r + 2 - 4 * ((r // 2) % 2)
+    along = r + 4 - 8 * (r // 4)
+    corner = across + 4 - 8 * (r // 4)
+
+    def mate(row):
+        return row + 1 - 2 * (row % 2)
+
+    own_f = pltpu.make_async_copy(f_ref, fall.at[c], own_sem)
+    own_f.start()
+
+    barrier = pltpu.get_barrier_semaphore()
+    for row in (sib, across, along):
+        pl.semaphore_signal(barrier, inc=1, device_id=(row, c), device_id_type=MESH)
+
+    @pl.when(c > 0)
+    def _():
+        pl.semaphore_signal(barrier, inc=1, device_id=(r, c - 1), device_id_type=MESH)
+
+    @pl.when(c < cols - 1)
+    def _():
+        pl.semaphore_signal(barrier, inc=1, device_id=(r, c + 1), device_id_type=MESH)
+
+    hp[r] = hp_ref[...]
+    l0[r, c] = lh_ref[0]
+    l1[r, c] = lh_ref[1:3]
+    pl.semaphore_wait(barrier, 3 + jnp.minimum(c, 1) + jnp.minimum(cols - 1 - c, 1))
+
+    def z_copy(piece, kind, way, t, part, sending):
+        shard = (c - t if way == 0 else c + t) if sending else (c - 1 - t if way == 0 else c + 1 + t)
+        target = c + 1 if way == 0 else c - 1
+        ref = piece(shard, part)
+        return pltpu.make_async_remote_copy(
+            ref, ref, z_send.at[kind, way, t, part], z_recv.at[kind, way, t, part],
+            device_id=(r, target), device_id_type=MESH,
+        )
+
+    def z_sends(way, t):
+        return (c < cols - 1) & (c - t >= 0) if way == 0 else (c > 0) & (c + t < cols)
+
+    def z_receives(way, t):
+        return c - 1 - t >= 0 if way == 0 else c + 1 + t < cols
+
+    def z_start(piece, kind, t, part):
+        for way in (0, 1):
+            @pl.when(z_sends(way, t))
+            def _():
+                z_copy(piece, kind, way, t, part, True).start()
+
+    def z_arrive(piece, kind, t, part):
+        for way in (0, 1):
+            @pl.when(z_receives(way, t))
+            def _():
+                z_copy(piece, kind, way, t, part, False).wait_recv()
+
+    def z_drain(piece, kind):
+        for t in range(cols - 1):
+            for part in (0, 1):
+                for way in (0, 1):
+                    @pl.when(z_sends(way, t))
+                    def _():
+                        z_copy(piece, kind, way, t, part, True).wait_send()
+
+    def l_piece(shard, part):
+        return l0.at[r, shard] if part == 0 else l1.at[r, shard]
+
+    def f_piece(shard, part):
+        return fall.at[shard, part]
+
+    def ex_copy(buf, number, k, slot, target, half):
+        n = buf.shape[1] // 2
+        ref = buf.at[slot] if half is None else buf.at[slot, pl.ds(half * n, n)]
+        return pltpu.make_async_remote_copy(
+            ref, ref, ex_send.at[number, k], ex_recv.at[number, k], device_id=(target, c), device_id_type=MESH,
+        )
+
+    sends = (
+        (r, sib, None), (r, across, None), (r, along, None), (across, along, 0), (across, sib, None),
+        (along, across, 1), (along, sib, None), (corner, sib, 0), (corner, sib, 1),
+    )
+    lands = (
+        (sib, None), (across, None), (along, None), (corner, 0), (mate(across), None),
+        (corner, 1), (mate(along), None), (mate(corner), 0), (mate(corner), 1),
+    )
+
+    def ex_start(buf, number, *which):
+        for k in which:
+            slot, target, half = sends[k]
+            ex_copy(buf, number, k, slot, target, half).start()
+
+    def ex_arrive(buf, number, *which):
+        for k in which:
+            slot, half = lands[k]
+            ex_copy(buf, number, k, slot, sib, half).wait_recv()
+
+    def ex_pass(buf, number):
+        ex_arrive(buf, number, 1)
+        ex_start(buf, number, 3, 4)
+        ex_arrive(buf, number, 2)
+        ex_start(buf, number, 5, 6)
+
+    def ex_finish(buf, number):
+        ex_arrive(buf, number, 3)
+        ex_start(buf, number, 7)
+        ex_arrive(buf, number, 5)
+        ex_start(buf, number, 8)
+        ex_arrive(buf, number, 0, 4, 6, 7, 8)
+        for k in range(9):
+            slot, target, half = sends[k]
+            ex_copy(buf, number, k, slot, target, half).wait_send()
+
+    z_start(l_piece, 0, 0, 0)
+    z_start(l_piece, 0, 0, 1)
+    ex_start(hp, 0, 0, 1, 2)
+    for t in range(cols - 1):
+        for part in (0, 1):
+            z_arrive(l_piece, 0, t, part)
+            if t + 1 < cols - 1:
+                z_start(l_piece, 0, t + 1, part)
+    own_f.wait()
+    z_start(f_piece, 1, 0, 0)
+    z_start(f_piece, 1, 0, 1)
+    z_drain(l_piece, 0)
+
+    group = r // 2
+    place = pl.ds(pl.multiple_of((r % 2) * NB, NB), NB)
+    l0[r, group, :, place] = inverse(l0[r, group, :, place])
+    ex_start(l0, 1, 0, 1, 2)
+    l1[r, group, 1, :, place] = inverse(l1[r, group, 1, :, place])
+    ex_start(l1, 2, 0, 1, 2)
+    ex_pass(hp, 0)
+    ex_finish(hp, 0)
+
+    my_columns = ev_ref[:, pl.ds(pl.multiple_of(r * NB, NB), NB)]
+
+    @pl.loop(0, 8)
+    def _(b):
+        for p in (0, 1):
+            rhs[p, pl.ds(pl.multiple_of(b * NB, NB), NB)] = matern(hp[b, p], my_columns)
+
+    ex_pass(l0, 1)
+    step = 32
+
+    @pl.loop(0, tail_out.shape[0] // step)
+    def _(m):
+        rows = pl.ds(pl.multiple_of(m * step, step), step)
+        tail_out[rows] = matern(tp_ref[rows], ev_ref[...])
+
+    ex_finish(l0, 1)
+
+    def solve(p, triangle, solved):
+        for g in range(4):
+            a, b = 2 * g, 2 * g + 1
+            xa = dot(triangle(a, g)[:, :NB], rhs[p, a * NB : a * NB + NB])
+            right = rhs[p, b * NB : b * NB + NB] - dot(triangle(b, g)[:, :NB], xa)
+            xb = dot(triangle(b, g)[:, NB:], right)
+            solved[r, a * NB : a * NB + NB] = xa
+            solved[r, b * NB : b * NB + NB] = xb
+            if g < 3:
+                xg = jnp.concatenate([xa, xb], 0)
+                for i in range(b + 1, 8):
+                    rhs[p, i * NB : i * NB + NB] -= dot(triangle(i, g), xg)
+
+    solve(0, lambda i, g: l0[i, g], x0)
+    z_arrive(f_piece, 1, 0, 0)
+    z_start(f_piece, 1, 1, 0)
+    ex_pass(l1, 2)
+    ex_finish(l1, 2)
+    ex_start(x0, 3, 0, 1, 2)
+
+    @pl.loop(0, 8)
+    def _(i):
+        rows = pl.ds(pl.multiple_of(i * NB, NB), NB)
+        total = rhs[1, rows]
+        for g in range(4):
+            total = total - dot(l1[i, g, 0], x0[r, g * 256 : g * 256 + 256])
+        rhs[1, rows] = total
+
+    z_arrive(f_piece, 1, 0, 1)
+    z_start(f_piece, 1, 1, 1)
+    ex_pass(x0, 3)
+    solve(1, lambda i, g: l1[i, g, 1], x1)
+    ex_start(x1, 4, 0, 1, 2)
+    ex_finish(x0, 3)
+
+    def spread_out(p, solved):
+        for b in range(8):
+            value = solved[b]
+            high = value.astype(jnp.bfloat16)
+            xhi[p, :, b * NB : b * NB + NB] = high
+            xlo[p, :, b * NB : b * NB + NB] = (value - high.astype(jnp.float32)).astype(jnp.bfloat16)
+            head_out[p, :, b * NB : b * NB + NB] = solved[b, pl.ds(pl.multiple_of(r * NB, NB), NB)]
+
+    def update(shard, p):
+        @pl.loop(0, 4)
+        def _(m):
+            rows = pl.ds(pl.multiple_of(m * 256, 256), 256)
+            deep = pl.ds(pl.multiple_of(shard * 256, 256), 256)
+            value = fall[shard, p, rows]
+            high = value.astype(jnp.bfloat16)
+            low = (value - high.astype(jnp.float32)).astype(jnp.bfloat16)
+            right = xhi[p, deep]
+            total = jnp.dot(high, right, preferred_element_type=jnp.float32)
+            total = total + jnp.dot(low, right, preferred_element_type=jnp.float32)
+            total = total + jnp.dot(high, xlo[p, deep], preferred_element_type=jnp.float32)
+            tail_out[rows] -= total
+
+    spread_out(0, x0)
+    z_arrive(f_piece, 1, 1, 0)
+    z_start(f_piece, 1, 2, 0)
+    ex_pass(x1, 4)
+    ex_finish(x1, 4)
+    spread_out(1, x1)
+    z_arrive(f_piece, 1, 1, 1)
+    z_start(f_piece, 1, 2, 1)
+
+    @pl.loop(0, 2)
+    def _(p):
+        update(c, p)
+        for t in (0, 1):
+            for way in (0, 1):
+                @pl.when(z_receives(way, t))
+                def _():
+                    update(c - 1 - t if way == 0 else c + 1 + t, p)
+
+    for p in (0, 1):
+        z_arrive(f_piece, 1, 2, p)
+        for way in (0, 1):
+            @pl.when(z_receives(way, 2))
+            def _():
+                update(c - 3 if way == 0 else c + 3, p)
+    z_drain(f_piece, 1)
+
+
+def per_device_kernel(cols, head_points, tail_points, eval_points, length_scales, head_factor, tail_factor):
+    scale = length_scales[:, None]
+    dims = head_points.shape[0]
+    hp = jnp.transpose(head_points / scale[:, :, None], (1, 2, 0))
+    hp = jnp.pad(hp, ((0, 0), (0, 0), (0, NB - dims)))
+    tp = jnp.transpose(tail_points / scale)
+    ev = eval_points / scale
+    lh = jnp.stack([head_factor[0, :, 0], head_factor[1, :, 0], head_factor[1, :, 1]])
+    f = jnp.transpose(tail_factor, (1, 0, 2))
+    tail, wide = tail_points.shape[1], eval_points.shape[1]
+    vmem = pl.BlockSpec(memory_space=pltpu.VMEM)
+    f32 = jnp.float32
+    return pl.pallas_call(
+        functools.partial(kernel, cols),
+        out_shape=(jax.ShapeDtypeStruct((2, NB, wide), f32), jax.ShapeDtypeStruct((tail, wide), f32)),
+        in_specs=[vmem, vmem, vmem, vmem, pl.BlockSpec(memory_space=pl.ANY)],
+        out_specs=(vmem, vmem),
+        scratch_shapes=[
+            pltpu.VMEM((8, 2, NB, NB), f32),
+            pltpu.VMEM((8, cols, NB, 256), f32),
+            pltpu.VMEM((8, cols, 2, NB, 256), f32),
+            pltpu.VMEM((8, 1024, NB), f32),
+            pltpu.VMEM((8, 1024, NB), f32),
+            pltpu.VMEM((2, 1024, NB), f32),
+            pltpu.VMEM((cols, 2, tail, 256), f32),
+            pltpu.VMEM((2, 1024, wide), jnp.bfloat16),
+            pltpu.VMEM((2, 1024, wide), jnp.bfloat16),
+            pltpu.SemaphoreType.DMA,
+            pltpu.SemaphoreType.DMA((5, 9)),
+            pltpu.SemaphoreType.DMA((5, 9)),
+            pltpu.SemaphoreType.DMA((2, 2, 3, 2)),
+            pltpu.SemaphoreType.DMA((2, 2, 3, 2)),
+        ],
+        compiler_params=pltpu.CompilerParams(
+            collective_id=0, has_side_effects=True, vmem_limit_bytes=60 * 1024 * 1024
+        ),
+    )(hp, tp, ev, lh, f)
 
 
 def kernel_block(row_points, col_points, length_scales):
@@ -15,25 +331,16 @@
     return (1.0 + scaled + scaled * scaled / 3.0) * jnp.exp(-scaled)
 
 
-def whole_triangle(block):
+def solve_panel(block, right_side):
     band = lax.all_gather(block, "col", axis=1, tiled=True)
-    return lax.all_gather(band, "row", axis=0, tiled=True)
-
-
-def solve_panel(block, right_side):
-    triangle = whole_triangle(block)
+    triangle = lax.all_gather(band, "row", axis=0, tiled=True)
     spread = lax.all_to_all(right_side, "row", split_axis=1, concat_axis=0, tiled=True)
     partial_value = jax.scipy.linalg.solve_triangular(triangle, spread, lower=True)
     return lax.all_gather(partial_value, "row", axis=1, tiled=True)
 
 
 def apply_panel(rows_factor, solved):
-    return jnp.dot(
-        lax.all_gather(rows_factor, "col", axis=1, tiled=True),
-        solved,
-        precision=lax.Precision.HIGHEST,
-        preferred_element_type=jnp.float32,
-    )
+    return dot(lax.all_gather(rows_factor, "col", axis=1, tiled=True), solved)
 
 
 def per_device(head_points, tail_points, eval_points, length_scales, head_factor, tail_factor):
@@ -63,8 +370,9 @@
         P(None, "row", None, "col"),
         P("row", None, "col"),
     )
+    fits = mesh.shape["row"] == 8 and mesh.shape["col"] == 4
     return jax.shard_map(
-        per_device,
+        functools.partial(per_device_kernel, mesh.shape["col"]) if fits else per_device,
         mesh=mesh,
         in_specs=placed,
         out_specs=(P(None, "row", "col"), P("row", "col")),

time: 495 us -> 202 us (0.41)
  Pallas kernels: 0 us -> 186 us
  other arithmetic: 182 us -> 3.2 us
  matrix products: 93.9 us -> 0 us
  waiting for transfers between devices: 92.3 us -> 0 us
  local copies, waits for them, and re-layouts: 64.1 us -> 11.9 us
  blocking collectives: 35.2 us -> 0 us
  between operations: 14.8 us -> 0.68 us
  starting transfers between devices: 7.71 us -> 0 us
    pallas_call x0 -> x1, Pallas kernels: none -> 186 us  [per_device_kernel(): pl.pallas_call(functools.partial(kernel, cols), out_shape=(jax.ShapeDtype...]
    another operation x6 -> x1, other arithmetic: 168 us -> 0.79 us  [per_device_kernel(): jnp.stack([head_factor[0, :, 0], head_factor[1, :, 0], head_factor[1, :,...]
    all_gather x6 -> x0, waiting for transfers between devices: 92.2 us -> none  [the longest x2 75.4 us: solve_panel(): return lax.all_gather(partial_value, 'row', axis=1, tiled=True)]
    dot_general x2 -> x0, matrix products: 70.7 us -> none  [apply_panel(): jnp.dot(lax.all_gather(rows_factor, 'col', axis=1, tiled=True), solved, p...]
    another operation x53 -> x1, local copies, waits for them, and re-layouts: 48.9 us -> 0.02 us  [per_device_kernel(): jnp.stack([head_factor[0, :, 0], head_factor[1, :, 0], head_factor[1, :,...]
    all_gather x2 -> x0, blocking collectives: 35.2 us -> none  [whole_triangle(): band = lax.all_gather(block, 'col', axis=1, tiled=True)]
    another operation x30 -> x0, matrix products: 23.3 us -> none  [solve_panel(): jax.scipy.linalg.solve_triangular(triangle, spread, lower=True)]
    all_to_all x2 -> x0, starting transfers between devices: 7.22 us -> none  [solve_panel(): lax.all_to_all(right_side, 'row', split_axis=1, concat_axis=0, tiled=True)]
  transfers between devices with their start and end apart: 8 -> 0, of which waited for: 4 -> 0; matrix products, arithmetic and copies ran while one was open for 57% -> 0% of each run, Pallas kernels for 0% -> 0%
where the time goes in v1:
time: 202 us; the launch traced here: 201 us
  Pallas kernels  186 us (92%)
  local copies, waits for them, and re-layouts  11.9 us (6%)
  other arithmetic  3.2 us (2%)
    pallas_call x1, Pallas kernels, per_device_kernel(): pl.pallas_call(functools.partial(kernel, cols), out_shape=(jax.ShapeDtype...  186 us
    unnamed x6, local copies, waits for them, and re-layouts  8.59 us

profile of v1, /device:TPU:0, one launch (start us, length us, event | category | flops | bytes accessed | tf_op | source)
XLA Modules:
  0.0 201.3 jit_solution(11485403546067659543)
XLA Ops:
  0.6 0.0 copy-start
  0.6 0.9 broadcast_divide_fusion.1
  1.6 1.5 broadcast_divide_fusion
  3.1 0.1 copy.16
  3.2 0.7 pad.4.hp_ref
  3.9 1.4 fusion
  5.4 0.8 pad_maximum_fusion.lh_ref
  6.1 1.0 copy.21.tp_ref
  7.1 0.0 copy-done
  7.1 1.5 copy.29
  8.6 185.5 %shard_map.77 = (f32[2,128,1024]{2,1,0:T(8,128)}, f32[1024,1024]{1,0:T(8,128)}) custom-call(f32[2,128,128]{2,1,0:T(8,128)} %pad.4.hp_ref, f32[1024,8]{1,0:T(8,128)} %copy.21.tp_ref, f32[8,1024]{1,0:T(8,128)} %get-tuple-element.5.ev_ref, f32[3,128,256]{2,1,0:T(8,128)} %pad_maximum_fusion.lh_ref, f32[2,1024,256]{2,1,0:T(8,128)} %bitcast.13), custom_call_target="tpu_custom_call" | custom-call | tf_op jit(solution)/shard_map/pallas_call | solution.py:296
  194.2 2.3 %copy.33 = f32[2,128,1024]{2,1,0:T(8,128)} copy(f32[2,128,1024]{2,1,0:T(8,128)} %get-tuple-element.11) | data formatting | bytes 2097152
  196.5 4.8 %copy.34 = f32[1024,1024]{1,0:T(8,128)} copy(f32[1024,1024]{1,0:T(8,128)} %get-tuple-element.12) | data formatting | bytes 8388608
  (2 shorter events, 0.0 us)
Async XLA Ops:
  0.6 6.5 %copy-start = (f32[1024,2,256]{2,1,0:T(2,128)S(1)}, f32[1024,2,256]{2,1,0:T(2,128)}, u32[]{:S(2)}) copy-start(f32[1024,2,256]{2,1,0:T(2,128)} %param.11) | copy-start | bytes 6291460

commit v2 on v1

--- a/solution.py
+++ b/solution.py
@@ -10,16 +10,17 @@
 MESH = pl.DeviceIdType.MESH
 HIGHEST = lax.Precision.HIGHEST
 NB = 128
+PARTS = 4
 
 
 def dot(a, b):
     return jnp.dot(a, b, precision=HIGHEST, preferred_element_type=jnp.float32)
 
 
-def matern(rows, columns):
+def matern(rows, columns, scales):
     total = jnp.zeros((rows.shape[0], columns.shape[1]), jnp.float32)
     for d in range(columns.shape[0]):
-        spread = rows[:, d : d + 1] - columns[d : d + 1, :]
+        spread = rows[:, d : d + 1] / scales[d] - columns[d : d + 1, :] / scales[d]
         total = total + spread * spread
     s = jnp.sqrt(5.0 * total)
     return (1.0 + s + s * s * (1.0 / 3.0)) * jnp.exp(-s)
@@ -42,8 +43,9 @@
 
 
 def kernel(
-    cols, hp_ref, tp_ref, ev_ref, lh_ref, f_ref, head_out, tail_out,
-    hp, l0, l1, x0, x1, rhs, fall, xhi, xlo, own_sem, ex_send, ex_recv, z_send, z_recv,
+    cols, hp_ref, tp_ref, ev_ref, scale_ref, lh_ref, f_ref, head_out, tail_out,
+    hp, l0, l1, x0, x1, rhs, fall, xhi, xlo, tail, head, tp,
+    own_sem, out_sem, ex_send, ex_recv, z_send, z_recv,
 ):
     r = lax.axis_index("row")
     c = lax.axis_index("col")
@@ -70,9 +72,16 @@
     def _():
         pl.semaphore_signal(barrier, inc=1, device_id=(r, c + 1), device_id_type=MESH)
 
-    hp[r] = hp_ref[...]
-    l0[r, c] = lh_ref[0]
-    l1[r, c] = lh_ref[1:3]
+    scales = [scale_ref[d] for d in range(ev_ref.shape[0])]
+
+    def block(p, q):
+        return jnp.concatenate([lh_ref[pl.ds(p * 4 * NB + 2 * half + q, NB, stride=4), :] for half in (0, 1)], 1)
+
+    l0[r, c] = block(0, 0)
+    l1[r, c, 0] = block(1, 0)
+    l1[r, c, 1] = block(1, 1)
+    for p in (0, 1):
+        hp[r, p] = hp_ref[pl.ds(p, ev_ref.shape[0], stride=2), :]
     pl.semaphore_wait(barrier, 3 + jnp.minimum(c, 1) + jnp.minimum(cols - 1 - c, 1))
 
     def z_copy(piece, kind, way, t, part, sending):
@@ -102,9 +111,9 @@
             def _():
                 z_copy(piece, kind, way, t, part, False).wait_recv()
 
-    def z_drain(piece, kind):
+    def z_drain(piece, kind, parts):
         for t in range(cols - 1):
-            for part in (0, 1):
+            for part in range(parts):
                 for way in (0, 1):
                     @pl.when(z_sends(way, t))
                     def _():
@@ -167,9 +176,13 @@
             if t + 1 < cols - 1:
                 z_start(l_piece, 0, t + 1, part)
     own_f.wait()
-    z_start(f_piece, 1, 0, 0)
-    z_start(f_piece, 1, 0, 1)
-    z_drain(l_piece, 0)
+    for part in range(PARTS):
+        z_start(f_piece, 1, 0, part)
+    z_drain(l_piece, 0, 2)
+
+    def pass_on(t, part):
+        z_arrive(f_piece, 1, t, part)
+        z_start(f_piece, 1, t + 1, part)
 
     group = r // 2
     place = pl.ds(pl.multiple_of((r % 2) * NB, NB), NB)
@@ -185,17 +198,20 @@
     @pl.loop(0, 8)
     def _(b):
         for p in (0, 1):
-            rhs[p, pl.ds(pl.multiple_of(b * NB, NB), NB)] = matern(hp[b, p], my_columns)
+            rhs[p, pl.ds(pl.multiple_of(b * NB, NB), NB)] = matern(jnp.transpose(hp[b, p]), my_columns, scales)
 
     ex_pass(l0, 1)
     step = 32
-
-    @pl.loop(0, tail_out.shape[0] // step)
+    for b in range(tp.shape[0] // NB):
+        tp[b * NB : b * NB + NB] = jnp.transpose(tp_ref[:, b * NB : b * NB + NB])
+
+    @pl.loop(0, tail.shape[0] // step)
     def _(m):
         rows = pl.ds(pl.multiple_of(m * step, step), step)
-        tail_out[rows] = matern(tp_ref[rows], ev_ref[...])
+        tail[rows] = matern(tp[rows], ev_ref[...], scales)
 
     ex_finish(l0, 1)
+    pass_on(0, 0)
 
     def solve(p, triangle, solved):
         for g in range(4):
@@ -211,11 +227,11 @@
                     rhs[p, i * NB : i * NB + NB] -= dot(triangle(i, g), xg)
 
     solve(0, lambda i, g: l0[i, g], x0)
-    z_arrive(f_piece, 1, 0, 0)
-    z_start(f_piece, 1, 1, 0)
+    pass_on(0, 1)
     ex_pass(l1, 2)
+    ex_start(x0, 3, 0, 1, 2)
+    pass_on(0, 2)
     ex_finish(l1, 2)
-    ex_start(x0, 3, 0, 1, 2)
 
     @pl.loop(0, 8)
     def _(i):
@@ -225,11 +241,11 @@
             total = total - dot(l1[i, g, 0], x0[r, g * 256 : g * 256 + 256])
         rhs[1, rows] = total
 
-    z_arrive(f_piece, 1, 0, 1)
-    z_start(f_piece, 1, 1, 1)
+    pass_on(0, 3)
     ex_pass(x0, 3)
     solve(1, lambda i, g: l1[i, g, 1], x1)
     ex_start(x1, 4, 0, 1, 2)
+    pass_on(1, 0)
     ex_finish(x0, 3)
 
     def spread_out(p, solved):
@@ -238,86 +254,107 @@
             high = value.astype(jnp.bfloat16)
             xhi[p, :, b * NB : b * NB + NB] = high
             xlo[p, :, b * NB : b * NB + NB] = (value - high.astype(jnp.float32)).astype(jnp.bfloat16)
-            head_out[p, :, b * NB : b * NB + NB] = solved[b, pl.ds(pl.multiple_of(r * NB, NB), NB)]
-
-    def update(shard, p):
-        @pl.loop(0, 4)
-        def _(m):
-            rows = pl.ds(pl.multiple_of(m * 256, 256), 256)
-            deep = pl.ds(pl.multiple_of(shard * 256, 256), 256)
-            value = fall[shard, p, rows]
+            head[p, :, b * NB : b * NB + NB] = solved[b, pl.ds(pl.multiple_of(r * NB, NB), NB)]
+
+    def update(shard, part):
+        size = fall.shape[2] // 4
+        rows = pl.ds(pl.multiple_of(part * size, size), size)
+        deep = pl.ds(pl.multiple_of(shard * 256, 256), 256)
+        total = tail[rows]
+        for q in (0, 1):
+            value = jnp.concatenate(
+                [fall[shard, part, pl.ds(2 * half + q, size, stride=4), :] for half in (0, 1)], 1
+            )
             high = value.astype(jnp.bfloat16)
             low = (value - high.astype(jnp.float32)).astype(jnp.bfloat16)
-            right = xhi[p, deep]
-            total = jnp.dot(high, right, preferred_element_type=jnp.float32)
-            total = total + jnp.dot(low, right, preferred_element_type=jnp.float32)
-            total = total + jnp.dot(high, xlo[p, deep], preferred_element_type=jnp.float32)
-            tail_out[rows] -= total
+            right = xhi[q, deep]
+            total = total - jnp.dot(high, right, preferred_element_type=jnp.float32)
+            total = total - jnp.dot(low, right, preferred_element_type=jnp.float32)
+            total = total - jnp.dot(high, xlo[q, deep], preferred_element_type=jnp.float32)
+        tail[rows] = total
+
+    def tail_copy(part):
+        size = fall.shape[2] // 4
+        rows = pl.ds(part * size, size)
+        return pltpu.make_async_copy(tail.at[rows], tail_out.at[rows], out_sem.at[part])
 
     spread_out(0, x0)
-    z_arrive(f_piece, 1, 1, 0)
-    z_start(f_piece, 1, 2, 0)
+    pass_on(1, 1)
     ex_pass(x1, 4)
+    pass_on(1, 2)
     ex_finish(x1, 4)
+    pass_on(1, 3)
     spread_out(1, x1)
-    z_arrive(f_piece, 1, 1, 1)
-    z_start(f_piece, 1, 2, 1)
-
-    @pl.loop(0, 2)
-    def _(p):
-        update(c, p)
+    head_copy = pltpu.make_async_copy(head, head_out, out_sem.at[PARTS])
+    head_copy.start()
+
+    @pl.loop(0, PARTS)
+    def _(part):
+        update(c, part)
         for t in (0, 1):
             for way in (0, 1):
                 @pl.when(z_receives(way, t))
                 def _():
-                    update(c - 1 - t if way == 0 else c + 1 + t, p)
-
-    for p in (0, 1):
-        z_arrive(f_piece, 1, 2, p)
-        for way in (0, 1):
-            @pl.when(z_receives(way, 2))
-            def _():
-                update(c - 3 if way == 0 else c + 3, p)
-    z_drain(f_piece, 1)
+                    update(c - 1 - t if way == 0 else c + 1 + t, part)
+
+    for part in range(PARTS):
+        z_arrive(f_piece, 1, 2, part)
+
+        @pl.when((c == 0) | (c == cols - 1))
+        def _():
+            update(cols - 1 - c, part)
+
+        tail_copy(part).start()
+    z_drain(f_piece, 1, PARTS)
+    for part in range(PARTS):
+        tail_copy(part).wait()
+    head_copy.wait()
 
 
 def per_device_kernel(cols, head_points, tail_points, eval_points, length_scales, head_factor, tail_factor):
-    scale = length_scales[:, None]
     dims = head_points.shape[0]
-    hp = jnp.transpose(head_points / scale[:, :, None], (1, 2, 0))
-    hp = jnp.pad(hp, ((0, 0), (0, 0), (0, NB - dims)))
-    tp = jnp.transpose(tail_points / scale)
-    ev = eval_points / scale
-    lh = jnp.stack([head_factor[0, :, 0], head_factor[1, :, 0], head_factor[1, :, 1]])
-    f = jnp.transpose(tail_factor, (1, 0, 2))
     tail, wide = tail_points.shape[1], eval_points.shape[1]
+
+    def by_halves(factor):
+        parts = factor.reshape(-1, 2, 2, NB)
+        return jnp.transpose(parts, (0, 2, 1, 3)).reshape(-1, NB)
+
+    hp = head_points.reshape(2 * dims, NB)
+    lh = by_halves(head_factor)
+    f = by_halves(tail_factor).reshape(PARTS, 4 * tail // PARTS, NB)
     vmem = pl.BlockSpec(memory_space=pltpu.VMEM)
+    smem = pl.BlockSpec(memory_space=pltpu.SMEM)
+    anywhere = pl.BlockSpec(memory_space=pl.ANY)
     f32 = jnp.float32
     return pl.pallas_call(
         functools.partial(kernel, cols),
         out_shape=(jax.ShapeDtypeStruct((2, NB, wide), f32), jax.ShapeDtypeStruct((tail, wide), f32)),
-        in_specs=[vmem, vmem, vmem, vmem, pl.BlockSpec(memory_space=pl.ANY)],
-        out_specs=(vmem, vmem),
+        in_specs=[vmem, vmem, vmem, smem, vmem, anywhere],
+        out_specs=(anywhere, anywhere),
         scratch_shapes=[
-            pltpu.VMEM((8, 2, NB, NB), f32),
+            pltpu.VMEM((8, 2, dims, NB), f32),
             pltpu.VMEM((8, cols, NB, 256), f32),
             pltpu.VMEM((8, cols, 2, NB, 256), f32),
             pltpu.VMEM((8, 1024, NB), f32),
             pltpu.VMEM((8, 1024, NB), f32),
             pltpu.VMEM((2, 1024, NB), f32),
-            pltpu.VMEM((cols, 2, tail, 256), f32),
+            pltpu.VMEM((cols, PARTS, 4 * tail // PARTS, NB), f32),
             pltpu.VMEM((2, 1024, wide), jnp.bfloat16),
             pltpu.VMEM((2, 1024, wide), jnp.bfloat16),
+            pltpu.VMEM((tail, wide), f32),
+            pltpu.VMEM((2, NB, wide), f32),
+            pltpu.VMEM((tail, dims), f32),
             pltpu.SemaphoreType.DMA,
+            pltpu.SemaphoreType.DMA((PARTS + 1,)),
             pltpu.SemaphoreType.DMA((5, 9)),
             pltpu.SemaphoreType.DMA((5, 9)),
-            pltpu.SemaphoreType.DMA((2, 2, 3, 2)),
-            pltpu.SemaphoreType.DMA((2, 2, 3, 2)),
+            pltpu.SemaphoreType.DMA((2, 2, 3, PARTS)),
+            pltpu.SemaphoreType.DMA((2, 2, 3, PARTS)),
         ],
         compiler_params=pltpu.CompilerParams(
             collective_id=0, has_side_effects=True, vmem_limit_bytes=60 * 1024 * 1024
         ),
-    )(hp, tp, ev, lh, f)
+    )(hp, tail_points, eval_points, length_scales, lh, f)
 
 
 def kernel_block(row_points, col_points, length_scales):

time: 202 us -> 186 us (0.921)
  Pallas kernels: 186 us -> 178 us
  local copies, waits for them, and re-layouts: 11.9 us -> 7.09 us
  other arithmetic: 3.2 us -> 0 us
    pallas_call x1, Pallas kernels: 186 us -> 178 us  [per_device_kernel(): pl.pallas_call(functools.partial(kernel, cols), out_shape=(jax.ShapeDtype...]
    div x2 -> x0, other arithmetic: 2.41 us -> none  [the longest x1 1.48 us: per_device_kernel(): ev = eval_points / scale]
    unnamed x6 -> x2, local copies, waits for them, and re-layouts: 8.59 us -> 7.09 us
where the time goes in v2:
time: 186 us
  Pallas kernels  178 us (96%)
  local copies, waits for them, and re-layouts  7.09 us (4%)
    pallas_call x1, Pallas kernels, per_device_kernel(): pl.pallas_call(functools.partial(kernel, cols), out_shape=(jax.ShapeDtype...  178 us
    unnamed x2, local copies, waits for them, and re-layouts  7.09 us

profile of v2, /device:TPU:0, one launch (start us, length us, event | category | flops | bytes accessed | tf_op | source)
XLA Modules:
  0.0 186.1 jit_solution(3154309726455837920)
XLA Ops:
  0.6 178.4 %shard_map.77 = (f32[2,128,1024]{2,1,0:T(8,128)}, f32[1024,1024]{1,0:T(8,128)}) custom-call(f32[16,128]{1,0:T(8,128)} %bitcast.13, f32[8,1024]{1,0:T(8,128)} %tp_ref.1, f32[8,1024]{1,0:T(8,128)} %ev_ref.1, f32[8]{0:T(128)} %scale_ref.1, f32[1024,128]{1,0:T(8,128)} %bitcast.12, f32[4,1024,128]{2,1,0:T(8,128)} %bitcast.11), custom_call_target="tpu_custom_call" | custom-call | tf_op jit(solution)/shard_map/pallas_call | solution.py:329
  179.1 2.3 %copy.12 = f32[2,128,1024]{2,1,0:T(8,128)} copy(f32[2,128,1024]{2,1,0:T(8,128)} %get-tuple-element.4) | data formatting | bytes 2097152
  181.4 4.8 %copy.13 = f32[1024,1024]{1,0:T(8,128)} copy(f32[1024,1024]{1,0:T(8,128)} %get-tuple-element.5) | data formatting | bytes 8388608

commit v3 on v2

--- a/solution.py
+++ b/solution.py
@@ -250,16 +250,20 @@
 
     def spread_out(p, solved):
         for b in range(8):
-            value = solved[b]
-            high = value.astype(jnp.bfloat16)
-            xhi[p, :, b * NB : b * NB + NB] = high
-            xlo[p, :, b * NB : b * NB + NB] = (value - high.astype(jnp.float32)).astype(jnp.bfloat16)
             head[p, :, b * NB : b * NB + NB] = solved[b, pl.ds(pl.multiple_of(r * NB, NB), NB)]
+
+    def split(shard):
+        deep = pl.ds(pl.multiple_of(shard * 256, 256), 256)
+        for q, solved in ((0, x0), (1, x1)):
+            for b in range(8):
+                value = solved[b, deep]
+                high = value.astype(jnp.bfloat16)
+                xhi[q, :, b * NB : b * NB + NB] = high
+                xlo[q, :, b * NB : b * NB + NB] = (value - high.astype(jnp.float32)).astype(jnp.bfloat16)
 
     def update(shard, part):
         size = fall.shape[2] // 4
         rows = pl.ds(pl.multiple_of(part * size, size), size)
-        deep = pl.ds(pl.multiple_of(shard * 256, 256), 256)
         total = tail[rows]
         for q in (0, 1):
             value = jnp.concatenate(
@@ -267,10 +271,10 @@
             )
             high = value.astype(jnp.bfloat16)
             low = (value - high.astype(jnp.float32)).astype(jnp.bfloat16)
-            right = xhi[q, deep]
+            right = xhi[q]
             total = total - jnp.dot(high, right, preferred_element_type=jnp.float32)
             total = total - jnp.dot(low, right, preferred_element_type=jnp.float32)
-            total = total - jnp.dot(high, xlo[q, deep], preferred_element_type=jnp.float32)
+            total = total - jnp.dot(high, xlo[q], preferred_element_type=jnp.float32)
         tail[rows] = total
 
     def tail_copy(part):
@@ -288,15 +292,21 @@
     head_copy = pltpu.make_async_copy(head, head_out, out_sem.at[PARTS])
     head_copy.start()
 
-    @pl.loop(0, PARTS)
-    def _(part):
-        update(c, part)
-        for t in (0, 1):
-            for way in (0, 1):
-                @pl.when(z_receives(way, t))
-                def _():
-                    update(c - 1 - t if way == 0 else c + 1 + t, part)
-
+    def update_all(shard):
+        split(shard)
+
+        @pl.loop(0, PARTS)
+        def _(part):
+            update(shard, part)
+
+    update_all(c)
+    for t in (0, 1):
+        for way in (0, 1):
+            @pl.when(z_receives(way, t))
+            def _():
+                update_all(c - 1 - t if way == 0 else c + 1 + t)
+
+    split(cols - 1 - c)
     for part in range(PARTS):
         z_arrive(f_piece, 1, 2, part)
 
@@ -325,11 +335,12 @@
     vmem = pl.BlockSpec(memory_space=pltpu.VMEM)
     smem = pl.BlockSpec(memory_space=pltpu.SMEM)
     anywhere = pl.BlockSpec(memory_space=pl.ANY)
+    hbm = pl.BlockSpec(memory_space=pltpu.HBM)
     f32 = jnp.float32
     return pl.pallas_call(
         functools.partial(kernel, cols),
         out_shape=(jax.ShapeDtypeStruct((2, NB, wide), f32), jax.ShapeDtypeStruct((tail, wide), f32)),
-        in_specs=[vmem, vmem, vmem, smem, vmem, anywhere],
+        in_specs=[vmem, vmem, vmem, smem, vmem, hbm],
         out_specs=(anywhere, anywhere),
         scratch_shapes=[
             pltpu.VMEM((8, 2, dims, NB), f32),
@@ -339,8 +350,8 @@
             pltpu.VMEM((8, 1024, NB), f32),
             pltpu.VMEM((2, 1024, NB), f32),
             pltpu.VMEM((cols, PARTS, 4 * tail // PARTS, NB), f32),
-            pltpu.VMEM((2, 1024, wide), jnp.bfloat16),
-            pltpu.VMEM((2, 1024, wide), jnp.bfloat16),
+            pltpu.VMEM((2, 256, wide), jnp.bfloat16),
+            pltpu.VMEM((2, 256, wide), jnp.bfloat16),
             pltpu.VMEM((tail, wide), f32),
             pltpu.VMEM((2, NB, wide), f32),
             pltpu.VMEM((tail, dims), f32),
@@ -352,7 +363,7 @@
             pltpu.SemaphoreType.DMA((2, 2, 3, PARTS)),
         ],
         compiler_params=pltpu.CompilerParams(
-            collective_id=0, has_side_effects=True, vmem_limit_bytes=60 * 1024 * 1024
+            collective_id=0, has_side_effects=True, vmem_limit_bytes=44 * 1024 * 1024
         ),
     )(hp, tail_points, eval_points, length_scales, lh, f)
 

time: 186 us -> 187 us (level)
    unnamed x2 -> x14, local copies, waits for them, and re-layouts: 7.09 us -> 8.48 us
where the time goes in v3:
time: 187 us; the launch traced here: 186 us
  Pallas kernels  177 us (95%)
  local copies, waits for them, and re-layouts  8.48 us (5%)
    pallas_call x1, Pallas kernels, per_device_kernel(): pl.pallas_call(functools.partial(kernel, cols), out_shape=(jax.ShapeDtype...  177 us
    unnamed x14, local copies, waits for them, and re-layouts  8.48 us

profile of v3, /device:TPU:0, one launch (start us, length us, event | category | flops | bytes accessed | tf_op | source)
XLA Modules:
  0.0 186.2 jit_solution(13396443049181035429)
XLA Ops:
  0.6 0.0 copy-start
  0.6 1.6 copy-done
  2.2 0.0 copy-start.1
  2.2 1.0 copy-done.1
  3.3 0.0 copy-start.2
  3.3 0.8 copy-done.2
  4.0 0.0 copy-start.3
  4.0 0.8 copy-done.3
  4.8 0.0 copy-start.4
  4.8 0.7 copy-done.4
  5.5 0.0 copy-start.5
  5.5 0.7 copy-done.5
  6.1 177.1 %shard_map.77 = (f32[2,128,1024]{2,1,0:T(8,128)S(1)}, f32[1024,1024]{1,0:T(8,128)S(1)}) custom-call(f32[16,128]{1,0:T(8,128)S(1)} %bitcast.13, f32[8,1024]{1,0:T(8,128)S(1)} %copy-done.2, f32[8,1024]{1,0:T(8,128)S(1)} %copy-done.3, f32[8]{0:T(128)S(1)} %copy-done.5, f32[1024,128]{1,0:T(8,128)S(1)} %bitcast.12, f32[4,1024,128]{2,1,0:T(8,128)S(1)} %bitcast.11), custom_call_target="tpu_custom_call" | custom-call | tf_op jit(solution)/shard_map/pallas_call | solution.py:340
  183.2 1.0 copy.12
  184.2 2.0 %copy.13 = f32[1024,1024]{1,0:T(8,128)} copy(f32[1024,1024]{1,0:T(8,128)S(1)} %get-tuple-element.5) | data formatting | bytes 8388608
Async XLA Ops:
  0.6 1.6 copy-start
  2.2 1.0 copy-start.1
  3.3 0.8 copy-start.2
  4.0 0.8 copy-start.3
  4.8 0.7 copy-start.4
  5.5 0.7 copy-start.5

commit v4 on v3

--- a/solution.py
+++ b/solution.py
@@ -252,20 +252,19 @@
         for b in range(8):
             head[p, :, b * NB : b * NB + NB] = solved[b, pl.ds(pl.multiple_of(r * NB, NB), NB)]
 
-    def split(shard):
+    def split(shard, q):
         deep = pl.ds(pl.multiple_of(shard * 256, 256), 256)
-        for q, solved in ((0, x0), (1, x1)):
-            for b in range(8):
-                value = solved[b, deep]
-                high = value.astype(jnp.bfloat16)
-                xhi[q, :, b * NB : b * NB + NB] = high
-                xlo[q, :, b * NB : b * NB + NB] = (value - high.astype(jnp.float32)).astype(jnp.bfloat16)
-
-    def update(shard, part):
+        for b in range(8):
+            value = (x0, x1)[q][b, deep]
+            high = value.astype(jnp.bfloat16)
+            xhi[q, :, b * NB : b * NB + NB] = high
+            xlo[q, :, b * NB : b * NB + NB] = (value - high.astype(jnp.float32)).astype(jnp.bfloat16)
+
+    def update(shard, part, *panels):
         size = fall.shape[2] // 4
         rows = pl.ds(pl.multiple_of(part * size, size), size)
         total = tail[rows]
-        for q in (0, 1):
+        for q in panels:
             value = jnp.concatenate(
                 [fall[shard, part, pl.ds(2 * half + q, size, stride=4), :] for half in (0, 1)], 1
             )
@@ -277,42 +276,48 @@
             total = total - jnp.dot(high, xlo[q], preferred_element_type=jnp.float32)
         tail[rows] = total
 
+    def update_all(shard, *panels):
+        for q in panels:
+            split(shard, q)
+
+        @pl.loop(0, PARTS)
+        def _(part):
+            update(shard, part, *panels)
+
+    def update_from(t, *panels):
+        for way in (0, 1):
+            @pl.when(z_receives(way, t))
+            def _():
+                update_all(c - 1 - t if way == 0 else c + 1 + t, *panels)
+
     def tail_copy(part):
         size = fall.shape[2] // 4
         rows = pl.ds(part * size, size)
         return pltpu.make_async_copy(tail.at[rows], tail_out.at[rows], out_sem.at[part])
 
     spread_out(0, x0)
+    update_all(c, 0)
+    ex_pass(x1, 4)
     pass_on(1, 1)
-    ex_pass(x1, 4)
+    update_from(0, 0)
     pass_on(1, 2)
     ex_finish(x1, 4)
     pass_on(1, 3)
     spread_out(1, x1)
     head_copy = pltpu.make_async_copy(head, head_out, out_sem.at[PARTS])
     head_copy.start()
-
-    def update_all(shard):
-        split(shard)
-
-        @pl.loop(0, PARTS)
-        def _(part):
-            update(shard, part)
-
-    update_all(c)
-    for t in (0, 1):
-        for way in (0, 1):
-            @pl.when(z_receives(way, t))
-            def _():
-                update_all(c - 1 - t if way == 0 else c + 1 + t)
-
-    split(cols - 1 - c)
+    update_all(c, 1)
+    update_from(0, 1)
+    update_from(1, 0, 1)
+    for q in (0, 1):
+        split(cols - 1 - c, q)
+
     for part in range(PARTS):
         z_arrive(f_piece, 1, 2, part)
 
         @pl.when((c == 0) | (c == cols - 1))
         def _():
-            update(cols - 1 - c, part)
+            update(cols - 1 - c, part, 0, 1)
 
         tail_copy(part).start()
     z_drain(f_piece, 1, PARTS)
@@ -332,6 +337,7 @@
     hp = head_points.reshape(2 * dims, NB)
     lh = by_halves(head_factor)
     f = by_halves(tail_factor).reshape(PARTS, 4 * tail // PARTS, NB)
+    operands = (hp, tail_points, eval_points, length_scales, lh, f)
     vmem = pl.BlockSpec(memory_space=pltpu.VMEM)
     smem = pl.BlockSpec(memory_space=pltpu.SMEM)
     anywhere = pl.BlockSpec(memory_space=pl.ANY)
@@ -365,7 +371,7 @@
         compiler_params=pltpu.CompilerParams(
             collective_id=0, has_side_effects=True, vmem_limit_bytes=44 * 1024 * 1024
         ),
-    )(hp, tail_points, eval_points, length_scales, lh, f)
+    )(*(pltpu.with_memory_space_constraint(x, pltpu.HBM) for x in operands))
 
 
 def kernel_block(row_points, col_points, length_scales):

time: 187 us -> 181 us (0.968)
  local copies, waits for them, and re-layouts: 8.48 us -> 2.99 us
    unnamed x14 -> x2, local copies, waits for them, and re-layouts: 8.48 us -> 2.99 us
where the time goes in v4:
time: 181 us
  Pallas kernels  178 us (98%)
  local copies, waits for them, and re-layouts  2.99 us (2%)
    pallas_call x1, Pallas kernels, per_device_kernel(): pl.pallas_call(functools.partial(kernel, cols), out_shape=(jax.ShapeDtype...  178 us

profile of v4, /device:TPU:0, one launch (start us, length us, event | category | flops | bytes accessed | tf_op | source)
XLA Modules:
  0.0 181.2 jit_solution(4060558457613893401)
XLA Ops:
  0.6 177.5 %shard_map.77 = (f32[2,128,1024]{2,1,0:T(8,128)S(1)}, f32[1024,1024]{1,0:T(8,128)S(1)}) custom-call(f32[16,128]{1,0:T(8,128)} %bitcast.13, f32[8,1024]{1,0:T(8,128)} %tp_ref.1, f32[8,1024]{1,0:T(8,128)} %ev_ref.1, f32[8]{0:T(128)} %scale_ref.1, f32[1024,128]{1,0:T(8,128)} %bitcast.12, f32[4,1024,128]{2,1,0:T(8,128)} %bitcast.11), custom_call_target="tpu_custom_call" | custom-call | tf_op jit(solution)/shard_map/pallas_call | solution.py:346
  178.2 1.0 copy.12
  179.1 2.0 %copy.13 = f32[1024,1024]{1,0:T(8,128)} copy(f32[1024,1024]{1,0:T(8,128)S(1)} %get-tuple-element.5) | data formatting | bytes 8388608

commit v5 on v4

--- a/solution.py
+++ b/solution.py
@@ -243,9 +243,10 @@
 
     pass_on(0, 3)
     ex_pass(x0, 3)
+    pass_on(1, 0)
     solve(1, lambda i, g: l1[i, g, 1], x1)
     ex_start(x1, 4, 0, 1, 2)
-    pass_on(1, 0)
+    pass_on(1, 1)
     ex_finish(x0, 3)
 
     def spread_out(p, solved):
@@ -296,13 +297,12 @@
         return pltpu.make_async_copy(tail.at[rows], tail_out.at[rows], out_sem.at[part])
 
     spread_out(0, x0)
+    pass_on(1, 2)
     update_all(c, 0)
     ex_pass(x1, 4)
-    pass_on(1, 1)
+    pass_on(1, 3)
     update_from(0, 0)
-    pass_on(1, 2)
     ex_finish(x1, 4)
-    pass_on(1, 3)
     spread_out(1, x1)
     head_copy = pltpu.make_async_copy(head, head_out, out_sem.at[PARTS])
     head_copy.start()

time: 181 us -> 181 us (level)
  no operation moved by 1% of the time
where the time goes in v5:
time: 181 us
  Pallas kernels  178 us (98%)
  local copies, waits for them, and re-layouts  2.99 us (2%)
    pallas_call x1, Pallas kernels, per_device_kernel(): pl.pallas_call(functools.partial(kernel, cols), out_shape=(jax.ShapeDtype...  178 us

profile of v5, /device:TPU:0, one launch (start us, length us, event | category | flops | bytes accessed | tf_op | source)
XLA Modules:
  0.0 181.2 jit_solution(4348379119636803276)
XLA Ops:
  0.6 177.5 %shard_map.77 = (f32[2,128,1024]{2,1,0:T(8,128)S(1)}, f32[1024,1024]{1,0:T(8,128)S(1)}) custom-call(f32[16,128]{1,0:T(8,128)} %bitcast.13, f32[8,1024]{1,0:T(8,128)} %tp_ref.1, f32[8,1024]{1,0:T(8,128)} %ev_ref.1, f32[8]{0:T(128)} %scale_ref.1, f32[1024,128]{1,0:T(8,128)} %bitcast.12, f32[4,1024,128]{2,1,0:T(8,128)} %bitcast.11), custom_call_target="tpu_custom_call" | custom-call | tf_op jit(solution)/shard_map/pallas_call | solution.py:346
  178.2 1.0 copy.12
  179.1 2.0 %copy.13 = f32[1024,1024]{1,0:T(8,128)} copy(f32[1024,1024]{1,0:T(8,128)S(1)} %get-tuple-element.5) | data formatting | bytes 8388608
